TPU v7x, 128 devices: a whole 4x4x4 slice. The times are simulated.
128 devices in a mesh: fsdp: 8 (over x, z_hi), ctx: 16 (over z_lo, y, core).
Axes of the slice: x: 4, y: 4, z: 4 (z_hi: 2, z_lo: 2; z = z_hi * 2 + z_lo), core: 2. Of those that a mesh axis runs over, the one named last changes fastest.
Arguments:
- inputs: bfloat16 [65536, 640], P(('fsdp', 'ctx')), may hold values from -6 to 6
- cotangent: bfloat16 [65536, 640], P(('fsdp', 'ctx')), may hold values from -6 to 6
- query_weight: float32 [640, 1024], P(None, ('fsdp', 'ctx')), may hold values from -0.25 to 0.25
- key_weight: float32 [640, 256], P(('fsdp', 'ctx')), may hold values from -0.25 to 0.25
- value_weight: float32 [640, 256], P(('fsdp', 'ctx')), may hold values from -0.25 to 0.25
- output_weight: float32 [1024, 640], P(('fsdp', 'ctx')), may hold values from -0.375 to 0.375
- gate_weight: float32 [640, 2048], P(None, ('fsdp', 'ctx')), may hold values from -0.25 to 0.25
- up_weight: float32 [640, 2048], P(None, ('fsdp', 'ctx')), may hold values from -0.25 to 0.25
- down_weight: float32 [2048, 640], P(('fsdp', 'ctx')), may hold values from -0.125 to 0.125
- norm_gains: float32 [2, 640], P(None, ('fsdp', 'ctx')), may hold values from 0.5 to 1.5
- query_moment: float32 [640, 1024], P(None, ('fsdp', 'ctx')), may hold values from -614.4 to 614.4
- key_moment: float32 [640, 256], P(('fsdp', 'ctx')), may hold values from -1228.8 to 1228.8
- value_moment: float32 [640, 256], P(('fsdp', 'ctx')), may hold values from -1638.4 to 1638.4
- output_moment: float32 [1024, 640], P(('fsdp', 'ctx')), may hold values from -1638.4 to 1638.4
- gate_moment: float32 [640, 2048], P(None, ('fsdp', 'ctx')), may hold values from -2048 to 2048
- up_moment: float32 [640, 2048], P(None, ('fsdp', 'ctx')), may hold values from -2048 to 2048
- down_moment: float32 [2048, 640], P(('fsdp', 'ctx')), may hold values from -2457.6 to 2457.6
- gain_first: float32 [2, 640], P(None, ('fsdp', 'ctx')), may hold values from -115.2 to 115.2
- gain_second: float32 [2, 640], P(None, ('fsdp', 'ctx')), may hold values from 5.89824 to 262.144, as said below
Outputs:
- block_output: float32 [65536, 640], P(('fsdp', 'ctx'))
- input_grad: float32 [65536, 640], P(('fsdp', 'ctx'))
- query_grad: float32 [640, 1024], P(None, ('fsdp', 'ctx'))
- key_grad: float32 [640, 256], P(('fsdp', 'ctx'))
- value_grad: float32 [640, 256], P(('fsdp', 'ctx'))
- output_grad: float32 [1024, 640], P(('fsdp', 'ctx'))
- gate_grad: float32 [640, 2048], P(None, ('fsdp', 'ctx'))
- up_grad: float32 [640, 2048], P(None, ('fsdp', 'ctx'))
- down_grad: float32 [2048, 640], P(('fsdp', 'ctx'))
- query_momentum: float32 [640, 1024], P(None, ('fsdp', 'ctx'))
- key_momentum: float32 [640, 256], P(('fsdp', 'ctx'))
- value_momentum: float32 [640, 256], P(('fsdp', 'ctx'))
- output_momentum: float32 [1024, 640], P(('fsdp', 'ctx'))
- gate_momentum: float32 [640, 2048], P(None, ('fsdp', 'ctx'))
- up_momentum: float32 [640, 2048], P(None, ('fsdp', 'ctx'))
- down_momentum: float32 [2048, 640], P(('fsdp', 'ctx'))
- query_updated: float32 [640, 1024], P(None, ('fsdp', 'ctx'))
- key_updated: float32 [640, 256], P(('fsdp', 'ctx'))
- value_updated: float32 [640, 256], P(('fsdp', 'ctx'))
- output_updated: float32 [1024, 640], P(('fsdp', 'ctx'))
- gate_updated: float32 [640, 2048], P(None, ('fsdp', 'ctx'))
- up_updated: float32 [640, 2048], P(None, ('fsdp', 'ctx'))
- down_updated: float32 [2048, 640], P(('fsdp', 'ctx'))
- gain_grads: float32 [2, 640], P(None, ('fsdp', 'ctx'))
- first_moments: float32 [2, 640], P(None, ('fsdp', 'ctx'))
- second_moments: float32 [2, 640], P(None, ('fsdp', 'ctx'))
- gains_updated: float32 [2, 640], P(None, ('fsdp', 'ctx'))
Inputs may be any that keep to these rules, and one draw needn't show every extreme that they name: `gain_second`: positive.
All inputs are finite; a program needn't handle non-finite values.
Results may differ from a plain program's by a relative error of at most 0.013.
The roundings to bfloat16 on the way count: a program that leaves them out, or rounds other values in their place, can miss the bound.
Values may be sent and summed in bfloat16 or wider, within the bound.
A program may use at most 192 MiB of HBM per device.

v0:
```python
import math

import jax
import jax.numpy as jnp
from jax import lax
from jax.sharding import PartitionSpec as P

HQ = 4
HD = 256
WINDOW = 512
NS_ITERS = 4
ADAM_STEP = 10


HIGH = lax.Precision.HIGHEST
NORM_EPS = 1e-06
ORTHO_EPS = 1e-07
POLY_FIRST = 3.4445
POLY_SECOND = -4.775
POLY_THIRD = 2.0315
MOMENTUM = 0.95
MUON_RATE = 0.6
MUON_DECAY = 0.01
ADAM_RATE = 0.7
BETA_FIRST = 0.9
BETA_SECOND = 0.999
ADAM_EPS = 1e-08
SHARD_DIMS = (1, 0, 0, 0, 1, 1, 0)


def from_behind(array, axis, by):
    length = lax.axis_size(axis)
    pairs = [(i, i + by) for i in range(length) if 0 <= i + by < length]
    return lax.ppermute(array, axis, pairs)


def rms_scale(values, gain_row):
    mean_square = jnp.mean(values * values, axis=-1, keepdims=True)
    return values * lax.rsqrt(mean_square + NORM_EPS) * gain_row


def gelu_product(gate_values, up_values):
    return jax.nn.gelu(gate_values, approximate=True) * up_values


def local_gram(current, shard_dim):
    if shard_dim == 1:
        return jnp.dot(current, current.T, precision=HIGH)
    return jnp.dot(current.T, current, precision=HIGH)


def sharded_grams(currents):
    partial_grams = [
        local_gram(current, shard_dim) for current, shard_dim in zip(currents, SHARD_DIMS)
    ]
    return lax.psum(
        (
            partial_grams[0],
            partial_grams[1],
            partial_grams[2],
            partial_grams[3],
            partial_grams[4],
            partial_grams[5],
            partial_grams[6],
        ),
        ("fsdp", "ctx"),
    )


def poly_step(current, gram_matrix, shard_dim):
    if shard_dim == 1:
        product = jnp.dot(gram_matrix, current, precision=HIGH)
        return (
            POLY_FIRST * current
            + POLY_SECOND * product
            + POLY_THIRD * jnp.dot(gram_matrix, product, precision=HIGH)
        )
    product = jnp.dot(current, gram_matrix, precision=HIGH)
    return (
        POLY_FIRST * current
        + POLY_SECOND * product
        + POLY_THIRD * jnp.dot(product, gram_matrix, precision=HIGH)
    )


def body(
    inputs,
    cotangent,
    query_weight,
    key_weight,
    value_weight,
    output_weight,
    gate_weight,
    up_weight,
    down_weight,
    norm_gains,
    query_moment,
    key_moment,
    value_moment,
    output_moment,
    gate_moment,
    up_moment,
    down_moment,
    gain_first,
    gain_second,
):
    query_full, key_full, value_full, output_full, gate_full, up_full, down_full, gains_full = (
        lax.all_gather(query_weight.astype(jnp.bfloat16), ("fsdp", "ctx"), axis=1, tiled=True),
        lax.all_gather(key_weight.astype(jnp.bfloat16), ("fsdp", "ctx"), axis=0, tiled=True),
        lax.all_gather(value_weight.astype(jnp.bfloat16), ("fsdp", "ctx"), axis=0, tiled=True),
        lax.all_gather(output_weight.astype(jnp.bfloat16), ("fsdp", "ctx"), axis=0, tiled=True),
        lax.all_gather(gate_weight.astype(jnp.bfloat16), ("fsdp", "ctx"), axis=1, tiled=True),
        lax.all_gather(up_weight.astype(jnp.bfloat16), ("fsdp", "ctx"), axis=1, tiled=True),
        lax.all_gather(down_weight.astype(jnp.bfloat16), ("fsdp", "ctx"), axis=0, tiled=True),
        lax.all_gather(norm_gains.astype(jnp.bfloat16), ("fsdp", "ctx"), axis=1, tiled=True),
    )
    token_count = inputs.shape[0]
    residual_in = inputs.astype(jnp.float32)
    attn_gain = gains_full[0].astype(jnp.float32)
    feed_gain = gains_full[1].astype(jnp.float32)
    first_normed, first_pullback = jax.vjp(rms_scale, residual_in, attn_gain)
    first_low = first_normed.astype(jnp.bfloat16)
    query_rows = (
        jnp.dot(first_low, query_full, preferred_element_type=jnp.float32)
        .astype(jnp.bfloat16)
        .reshape(token_count, HQ, HD)
    )
    key_value = jnp.dot(
        first_low,
        jnp.concatenate([key_full, value_full], axis=1),
        preferred_element_type=jnp.float32,
    ).astype(jnp.bfloat16)
    reach_count = (WINDOW + token_count - 2) // token_count
    earlier = [from_behind(key_value, "ctx", 1)]
    window_rows = jnp.concatenate(earlier + [key_value], axis=0)
    key_rows = window_rows[:, :HD]
    value_rows = window_rows[:, HD:]
    first_position = lax.axis_index("ctx") * token_count
    query_position = first_position + jnp.arange(token_count, dtype=jnp.int32)
    key_position = (
        first_position
        - reach_count * token_count
        + jnp.arange((reach_count + 1) * token_count, dtype=jnp.int32)
    )
    allowed = (
        (key_position[None, :] <= query_position[:, None])
        & (key_position[None, :] > query_position[:, None] - WINDOW)
        & (key_position[None, :] >= 0)
    )
    score_scale = 1.0 / math.sqrt(HD)

    def masked_scores():
        raw_scores = (
            jnp.einsum("ihd,jd->hij", query_rows, key_rows, preferred_element_type=jnp.float32)
            * score_scale
        )
        return jnp.where(allowed[None], raw_scores, -jnp.inf)

    scores = masked_scores()
    row_max = jnp.max(scores, axis=-1, keepdims=True)
    exp_scores = jnp.exp(scores - row_max)
    row_total = jnp.sum(exp_scores, axis=-1, keepdims=True)
    log_total = row_max + jnp.log(row_total)
    prob_low = (exp_scores / row_total).astype(jnp.bfloat16)
    attended = jnp.einsum("hij,jd->ihd", prob_low, value_rows, preferred_element_type=jnp.float32)
    mixed_low = attended.reshape(token_count, HQ * HD).astype(jnp.bfloat16)
    middle = residual_in + jnp.dot(mixed_low, output_full, preferred_element_type=jnp.float32)
    second_normed, second_pullback = jax.vjp(rms_scale, middle, feed_gain)
    second_low = second_normed.astype(jnp.bfloat16)
    gate_values = jnp.dot(second_low, gate_full, preferred_element_type=jnp.float32)
    up_values = jnp.dot(second_low, up_full, preferred_element_type=jnp.float32)
    hidden_values, hidden_pullback = jax.vjp(gelu_product, gate_values, up_values)
    hidden_low = hidden_values.astype(jnp.bfloat16)
    block_output = middle + jnp.dot(hidden_low, down_full, preferred_element_type=jnp.float32)
    query_back, key_back, value_back, output_back, gate_back, up_back, down_back, gains_back = (
        lax.all_gather(query_weight.astype(jnp.bfloat16), ("fsdp", "ctx"), axis=1, tiled=True),
        lax.all_gather(key_weight.astype(jnp.bfloat16), ("fsdp", "ctx"), axis=0, tiled=True),
        lax.all_gather(value_weight.astype(jnp.bfloat16), ("fsdp", "ctx"), axis=0, tiled=True),
        lax.all_gather(output_weight.astype(jnp.bfloat16), ("fsdp", "ctx"), axis=0, tiled=True),
        lax.all_gather(gate_weight.astype(jnp.bfloat16), ("fsdp", "ctx"), axis=1, tiled=True),
        lax.all_gather(up_weight.astype(jnp.bfloat16), ("fsdp", "ctx"), axis=1, tiled=True),
        lax.all_gather(down_weight.astype(jnp.bfloat16), ("fsdp", "ctx"), axis=0, tiled=True),
        lax.all_gather(norm_gains.astype(jnp.bfloat16), ("fsdp", "ctx"), axis=1, tiled=True),
    )
    hidden_cot = jnp.dot(cotangent, down_back.T, preferred_element_type=jnp.float32)
    down_local = jnp.dot(hidden_low.T, cotangent, preferred_element_type=jnp.float32)
    gate_cot, up_cot = hidden_pullback(hidden_cot)
    gate_low = gate_cot.astype(jnp.bfloat16)
    up_low = up_cot.astype(jnp.bfloat16)
    gate_local = jnp.dot(second_low.T, gate_low, preferred_element_type=jnp.float32)
    up_local = jnp.dot(second_low.T, up_low, preferred_element_type=jnp.float32)
    second_cot = jnp.dot(gate_low, gate_back.T, preferred_element_type=jnp.float32) + jnp.dot(
        up_low, up_back.T, preferred_element_type=jnp.float32
    )
    middle_part, feed_gain_cot = second_pullback(second_cot)
    middle_cot = cotangent.astype(jnp.float32) + middle_part
    middle_low = middle_cot.astype(jnp.bfloat16)
    output_local = jnp.dot(mixed_low.T, middle_low, preferred_element_type=jnp.float32)
    attended_cot = (
        jnp.dot(middle_low, output_back.T, preferred_element_type=jnp.float32)
        .astype(jnp.bfloat16)
        .reshape(token_count, HQ, HD)
    )
    prob_exact = jnp.exp(masked_scores() - log_total)
    prob_cot = jnp.einsum(
        "ihd,jd->hij", attended_cot, value_rows, preferred_element_type=jnp.float32
    )
    score_cot = prob_exact * (prob_cot - jnp.sum(prob_cot * prob_exact, axis=-1, keepdims=True))
    score_low = score_cot.astype(jnp.bfloat16)
    query_cot = (
        (
            jnp.einsum("hij,jd->ihd", score_low, key_rows, preferred_element_type=jnp.float32)
            * score_scale
        )
        .astype(jnp.bfloat16)
        .reshape(token_count, HQ * HD)
    )
    key_cot = (
        jnp.einsum("hij,ihd->jd", score_low, query_rows, preferred_element_type=jnp.float32)
        * score_scale
    )
    value_cot = jnp.einsum(
        "hij,ihd->jd",
        prob_exact.astype(jnp.bfloat16),
        attended_cot,
        preferred_element_type=jnp.float32,
    )
    window_cot = jnp.concatenate([key_cot, value_cot], axis=1)
    edge_total = window_cot[reach_count * token_count :]
    returned = from_behind(
        window_cot[(reach_count - 1) * token_count : (reach_count - 1 + 1) * token_count].astype(
            jnp.bfloat16
        ),
        "ctx",
        -1,
    ).astype(jnp.float32)
    edge_total = edge_total + returned
    edge_low = edge_total.astype(jnp.bfloat16)
    key_low = edge_low[:, :HD]
    value_low = edge_low[:, HD:]
    query_local = jnp.dot(first_low.T, query_cot, preferred_element_type=jnp.float32)
    key_local = jnp.dot(first_low.T, key_low, preferred_element_type=jnp.float32)
    value_local = jnp.dot(first_low.T, value_low, preferred_element_type=jnp.float32)
    first_cot = (
        jnp.dot(query_cot, query_back.T, preferred_element_type=jnp.float32)
        + jnp.dot(key_low, key_back.T, preferred_element_type=jnp.float32)
        + jnp.dot(value_low, value_back.T, preferred_element_type=jnp.float32)
    )
    input_part, attn_gain_cot = first_pullback(first_cot)
    input_grad = middle_cot + input_part
    reduced = (
        lax.psum_scatter(query_local, ("fsdp", "ctx"), scatter_dimension=1, tiled=True),
        lax.psum_scatter(key_local, ("fsdp", "ctx"), scatter_dimension=0, tiled=True),
        lax.psum_scatter(value_local, ("fsdp", "ctx"), scatter_dimension=0, tiled=True),
        lax.psum_scatter(output_local, ("fsdp", "ctx"), scatter_dimension=0, tiled=True),
        lax.psum_scatter(gate_local, ("fsdp", "ctx"), scatter_dimension=1, tiled=True),
        lax.psum_scatter(up_local, ("fsdp", "ctx"), scatter_dimension=1, tiled=True),
        lax.psum_scatter(down_local, ("fsdp", "ctx"), scatter_dimension=0, tiled=True),
        lax.psum_scatter(
            jnp.stack([attn_gain_cot, feed_gain_cot]),
            ("fsdp", "ctx"),
            scatter_dimension=1,
            tiled=True,
        ),
    )
    masters = (
        query_weight,
        key_weight,
        value_weight,
        output_weight,
        gate_weight,
        up_weight,
        down_weight,
    )
    moments = (
        query_moment,
        key_moment,
        value_moment,
        output_moment,
        gate_moment,
        up_moment,
        down_moment,
    )
    fresh = tuple(
        (MOMENTUM * old_moment + new_grad for old_moment, new_grad in zip(moments, reduced[:7]))
    )
    group_size = lax.axis_size(("fsdp", "ctx"))
    squares = lax.psum(
        (
            jnp.sum(fresh[0] * fresh[0]),
            jnp.sum(fresh[1] * fresh[1]),
            jnp.sum(fresh[2] * fresh[2]),
            jnp.sum(fresh[3] * fresh[3]),
            jnp.sum(fresh[4] * fresh[4]),
            jnp.sum(fresh[5] * fresh[5]),
            jnp.sum(fresh[6] * fresh[6]),
        ),
        ("fsdp", "ctx"),
    )
    factors = tuple((1.0 / (jnp.sqrt(square_sum) + ORTHO_EPS) for square_sum in squares))
    currents = tuple((moment_now * factor for moment_now, factor in zip(fresh, factors)))
    grams = sharded_grams(currents)
    for iteration in range(NS_ITERS):
        if iteration > 0:
            grams = sharded_grams(currents)
        currents = tuple(
            (
                poly_step(current, gram_matrix, shard_dim)
                for current, gram_matrix, shard_dim in zip(currents, grams, SHARD_DIMS)
            )
        )
    updated = []
    for master, orthogonal, shard_dim in zip(masters, currents, SHARD_DIMS):
        row_count = master.shape[0] * (group_size if shard_dim == 0 else 1)
        col_count = master.shape[1] * (group_size if shard_dim == 1 else 1)
        step_ratio = math.sqrt(max(row_count, col_count) / row_count)
        updated.append(
            master * (1.0 - MUON_RATE * MUON_DECAY) - MUON_RATE * step_ratio * orthogonal
        )
    gain_grads = reduced[7]
    first_moments = BETA_FIRST * gain_first + (1.0 - BETA_FIRST) * gain_grads
    second_moments = BETA_SECOND * gain_second + (1.0 - BETA_SECOND) * gain_grads * gain_grads
    first_hat = first_moments / (1.0 - BETA_FIRST**ADAM_STEP)
    second_hat = second_moments / (1.0 - BETA_SECOND**ADAM_STEP)
    gains_updated = norm_gains - ADAM_RATE * first_hat / (jnp.sqrt(second_hat) + ADAM_EPS)
    return (
        block_output,
        input_grad,
        reduced[0],
        reduced[1],
        reduced[2],
        reduced[3],
        reduced[4],
        reduced[5],
        reduced[6],
        fresh[0],
        fresh[1],
        fresh[2],
        fresh[3],
        fresh[4],
        fresh[5],
        fresh[6],
        updated[0],
        updated[1],
        updated[2],
        updated[3],
        updated[4],
        updated[5],
        updated[6],
        gain_grads,
        first_moments,
        second_moments,
        gains_updated,
    )


def solution(mesh):
    placed = (
        P(("fsdp", "ctx"), None),
        P(("fsdp", "ctx"), None),
        P(None, ("fsdp", "ctx")),
        P(("fsdp", "ctx"), None),
        P(("fsdp", "ctx"), None),
        P(("fsdp", "ctx"), None),
        P(None, ("fsdp", "ctx")),
        P(None, ("fsdp", "ctx")),
        P(("fsdp", "ctx"), None),
        P(None, ("fsdp", "ctx")),
        P(None, ("fsdp", "ctx")),
        P(("fsdp", "ctx"), None),
        P(("fsdp", "ctx"), None),
        P(("fsdp", "ctx"), None),
        P(None, ("fsdp", "ctx")),
        P(None, ("fsdp", "ctx")),
        P(("fsdp", "ctx"), None),
        P(None, ("fsdp", "ctx")),
        P(None, ("fsdp", "ctx")),
    )
    return jax.shard_map(
        body,
        mesh=mesh,
        in_specs=placed,
        out_specs=(
            P(("fsdp", "ctx"), None),
            P(("fsdp", "ctx"), None),
            P(None, ("fsdp", "ctx")),
            P(("fsdp", "ctx"), None),
            P(("fsdp", "ctx"), None),
            P(("fsdp", "ctx"), None),
            P(None, ("fsdp", "ctx")),
            P(None, ("fsdp", "ctx")),
            P(("fsdp", "ctx"), None),
            P(None, ("fsdp", "ctx")),
            P(("fsdp", "ctx"), None),
            P(("fsdp", "ctx"), None),
            P(("fsdp", "ctx"), None),
            P(None, ("fsdp", "ctx")),
            P(None, ("fsdp", "ctx")),
            P(("fsdp", "ctx"), None),
            P(None, ("fsdp", "ctx")),
            P(("fsdp", "ctx"), None),
            P(("fsdp", "ctx"), None),
            P(("fsdp", "ctx"), None),
            P(None, ("fsdp", "ctx")),
            P(None, ("fsdp", "ctx")),
            P(("fsdp", "ctx"), None),
            P(None, ("fsdp", "ctx")),
            P(None, ("fsdp", "ctx")),
            P(None, ("fsdp", "ctx")),
            P(None, ("fsdp", "ctx")),
        ),
        check_vma=False,
    )
```

profile of v0, /device:TPU:1, one launch (start us, length us, event | category | flops | bytes accessed | tf_op | source)
XLA Modules:
  0.0 3350.6 jit_solution(7809427699237686237)
XLA Ops:
  17.9 34.3 %all-gather = bf16[128,5,2]{1,2,0:T(2,128)(2,1)S(1)} all-gather(bf16[1,5,2]{1,2,0:T(2,128)(2,1)S(1)} %convert_bitcast_fusion.2), channel_id=1, replica_groups=mesh['fsdp'=8,'ctx'=16] {'fsdp','ctx'}, dimensions={0}, use_global_device_ids=true | all-gather | bytes 2580 | tf_op jit(solution)/shard_map/all_gather | solution.py:115
  52.5 33.6 %all-gather.2 = bf16[128,5,256]{2,1,0:T(8,128)(2,1)S(1)} all-gather(bf16[1,5,256]{2,1,0:T(8,128)(2,1)S(1)} %convert_bitcast_fusion), channel_id=1, replica_groups=mesh['fsdp'=8,'ctx'=16] {'fsdp','ctx'}, dimensions={0}, use_global_device_ids=true | all-gather | bytes 330240 | tf_op jit(solution)/shard_map/all_gather | solution.py:110
  86.3 34.2 %all-gather.1 = bf16[128,5,256]{2,1,0:T(8,128)(2,1)S(1)} all-gather(bf16[1,5,256]{2,1,0:T(8,128)(2,1)S(1)} %convert_bitcast_fusion.1), channel_id=1, replica_groups=mesh['fsdp'=8,'ctx'=16] {'fsdp','ctx'}, dimensions={0}, use_global_device_ids=true | all-gather | bytes 330240 | tf_op jit(solution)/shard_map/all_gather | solution.py:109
  138.8 5.1 all-gather.11.cloned.1.call-done
  146.7 64.1 %all-gather.15.cloned.1.call-done = bf16[640,2048]{0,1:T(8,128)(2,1)} async-done(((bf16[640,16]{0,1:T(8,128)(2,1)}), bf16[640,2048]{0,1:T(8,128)(2,1)}) %all-gather.15.cloned.1.call-update) | async-done | bytes 2621456 | tf_op jit(solution)/shard_map/all_gather | solution.py:113
  210.8 5.5 fusion.156
  216.3 61.0 %all-gather.13.cloned.1.call-done = bf16[640,2048]{0,1:T(8,128)(2,1)} async-done(((bf16[640,16]{0,1:T(8,128)(2,1)}), bf16[640,2048]{0,1:T(8,128)(2,1)}) %all-gather.13.cloned.1.call-update) | async-done | bytes 2621456 | tf_op jit(solution)/shard_map/all_gather | solution.py:112
  277.3 5.6 fusion.155
  282.9 60.9 %all-gather.17.cloned.1.call-done = bf16[2048,640]{1,0:T(8,128)(2,1)} async-done(((bf16[16,640]{1,0:T(8,128)(2,1)}), bf16[2048,640]{1,0:T(8,128)(2,1)}) %all-gather.17.cloned.1.call-update) | async-done | bytes 2621456 | tf_op jit(solution)/shard_map/all_gather | solution.py:114
  343.9 9.0 multiply_convert_fusion
  369.4 5.3 fusion
  392.0 5.8 fusion.161
  397.9 5.9 fusion.160
  403.9 5.8 fusion.159
  416.7 133.9 %all-reduce.25.cloned.1.call-done = (f32[640,1024]{0,1:T(8,128)}, f32[640,256]{1,0:T(8,128)}, f32[640,256]{1,0:T(8,128)}, f32[1024,640]{1,0:T(8,128)}) async-done(((f32[640,1024]{0,1:T(8,128)}, f32[640,256]{1,0:T(8,128)}, f32[640,256]{1,0:T(8,128)}, f32[1024,640]{1,0:T(8,128)}), (f32[640,1024]{0,1:T(8,128)}, f32[640,256]{1,0:T(8,128)}, f32[640,256]{1,0:T(8,128)}, ...) | async-done | bytes 6553616
  558.3 630.6 %reduce-scatter.9.cloned.1.call-done = f32[16,640]{1,0:T(8,128)} async-done(((f32[2048,640]{1,0:T(8,128)}), f32[16,640]{1,0:T(8,128)}) %reduce-scatter.9.cloned.1.call-update) | async-done | bytes 40976 | tf_op jit(solution)/shard_map/reduce_scatter | solution.py:258
  1190.4 639.1 %reduce-scatter.7.cloned.1.call-done = f32[640,16]{0,1:T(8,128)} async-done(((f32[640,2048]{0,1:T(8,128)}), f32[640,16]{0,1:T(8,128)}) %reduce-scatter.7.cloned.1.call-update) | async-done | bytes 40976 | tf_op jit(solution)/shard_map/reduce_scatter | solution.py:257
  1830.9 639.8 %reduce-scatter.5.cloned.1.call-done = f32[640,16]{0,1:T(8,128)} async-done(((f32[640,2048]{0,1:T(8,128)}), f32[640,16]{0,1:T(8,128)}) %reduce-scatter.5.cloned.1.call-update) | async-done | bytes 40976 | tf_op jit(solution)/shard_map/reduce_scatter | solution.py:256
  2472.0 69.7 %all-reduce.5 = (f32[]{:T(128)}, f32[]{:T(128)}, f32[]{:T(128)}, f32[]{:T(128)}, f32[]{:T(128)}, /*index=5*/f32[]{:T(128)}, f32[]{:T(128)}, f32[2,640]{1,0:T(2,128)}) all-reduce(f32[]{:T(128)} %get-tuple-element.92, f32[]{:T(128)} %get-tuple-element.89, f32[]{:T(128)} %get-tuple-element.86, ...), channel_id=1, replica_groups=mesh['fsdp'=8,'ctx'=16] {'fsdp','ctx'}, use_global_device_ids=true, to_apply=%region_15.16 | all-reduce | flops 1287 | bytes 10296 | tf_op jit(solution)/shard_map/psum | solution.py:288
  2563.1 161.2 %all-reduce.23.cloned.1.call-done = (f32[640,640]{1,0:T(8,128)}, f32[256,256]{1,0:T(8,128)}, f32[256,256]{1,0:T(8,128)}, f32[640,640]{1,0:T(8,128)}, f32[640,640...) async-done(((f32[640,640]{1,0:T(8,128)}, f32[256,256]{1,0:T(8,128)}, f32[256,256]{1,0:T(8,128)}, f32[640,640]{1,0:T(8,128)}, f32[640,640]{1,0:T(8,128)}, ...) | async-done | bytes 8716304 | tf_op jit(solution)/shard_map/psum | solution.py:56
  2759.6 163.3 %all-reduce.21.cloned.1.call-done = (f32[640,640]{1,0:T(8,128)}, f32[256,256]{1,0:T(8,128)}, f32[256,256]{1,0:T(8,128)}, f32[640,640]{1,0:T(8,128)}, f32[640,640...) async-done(((f32[640,640]{1,0:T(8,128)}, f32[256,256]{1,0:T(8,128)}, f32[256,256]{1,0:T(8,128)}, f32[640,640]{1,0:T(8,128)}, f32[640,640]{1,0:T(8,128)}, ...) | async-done | bytes 8716304 | tf_op jit(solution)/shard_map/psum | solution.py:56
  2958.5 163.1 %all-reduce.19.cloned.1.call-done = (f32[640,640]{1,0:T(8,128)}, f32[256,256]{1,0:T(8,128)}, f32[256,256]{1,0:T(8,128)}, f32[640,640]{1,0:T(8,128)}, f32[640,640...) async-done(((f32[640,640]{1,0:T(8,128)}, f32[256,256]{1,0:T(8,128)}, f32[256,256]{1,0:T(8,128)}, f32[640,640]{1,0:T(8,128)}, f32[640,640]{1,0:T(8,128)}, ...) | async-done | bytes 8716304 | tf_op jit(solution)/shard_map/psum | solution.py:56
  3158.1 5.3 convolution_add_fusion.3
  3166.3 153.8 %all-reduce.17.cloned.1.call-done = (f32[640,640]{1,0:T(8,128)}, f32[256,256]{1,0:T(8,128)}, f32[256,256]{1,0:T(8,128)}, f32[640,640]{1,0:T(8,128)}, f32[640,640...) async-done(((f32[640,640]{1,0:T(8,128)}, f32[256,256]{1,0:T(8,128)}, f32[256,256]{1,0:T(8,128)}, f32[640,640]{1,0:T(8,128)}, f32[640,640]{1,0:T(8,128)}, ...) | async-done | bytes 8716304 | tf_op jit(solution)/shard_map/psum | solution.py:56
  (339 shorter events, 234.3 us)
Async XLA Ops:
  7.2 118.4 %all-gather.9.cloned.1.call-start = ((), (), s32[]{:S(2)}) async-start(), calls=%async_computation.3 | async-start | bytes 1320960 | tf_op jit(solution)/shard_map/all_gather | solution.py:108
  8.6 135.4 %all-gather.11.cloned.1.call-start = ((), (), s32[]{:S(2)}) async-start(), calls=%async_computation.4 | async-start | bytes 1320960 | tf_op jit(solution)/shard_map/all_gather | solution.py:111
  10.0 200.8 %all-gather.15.cloned.1.call-start = ((), (), s32[]{:S(2)}) async-start(), calls=%async_computation.6 | async-start | bytes 2641920 | tf_op jit(solution)/shard_map/all_gather | solution.py:113
  11.5 265.9 %all-gather.13.cloned.1.call-start = ((), (), s32[]{:S(2)}) async-start(), calls=%async_computation.5 | async-start | bytes 2641920 | tf_op jit(solution)/shard_map/all_gather | solution.py:112
  12.9 330.9 %all-gather.17.cloned.1.call-start = ((), (), s32[]{:S(2)}) async-start(), calls=%async_computation.7 | async-start | bytes 2641920 | tf_op jit(solution)/shard_map/all_gather | solution.py:114
  14.4 536.2 %all-reduce.25.cloned.1.call-start = ((), (), s32[]{:S(2)}) async-start(), calls=%async_computation.15 | async-start | bytes 13107200
  121.3 9.0 collective-permute-start
  378.6 10.5 collective-permute-start.1
  392.0 797.0 %reduce-scatter.9.cloned.1.call-start = ((), (), s32[]{:S(2)}) async-start(), calls=%async_computation.10 | async-start | bytes 5283840 | tf_op jit(solution)/shard_map/reduce_scatter | solution.py:258
  397.9 1431.6 %reduce-scatter.7.cloned.1.call-start = ((), (), s32[]{:S(2)}) async-start(), calls=%async_computation.9 | async-start | bytes 5283840 | tf_op jit(solution)/shard_map/reduce_scatter | solution.py:257
  403.8 2066.8 %reduce-scatter.5.cloned.1.call-start = ((), (), s32[]{:S(2)}) async-start(), calls=%async_computation.8 | async-start | bytes 5283840 | tf_op jit(solution)/shard_map/reduce_scatter | solution.py:256
  409.7 2314.6 %all-reduce.23.cloned.1.call-start = ((), (), s32[]{:S(2)}) async-start(), calls=%async_computation.14 | async-start | bytes 17432576 | tf_op jit(solution)/shard_map/psum | solution.py:56
  414.4 774.5 %copy-start.55 = (f32[16,640]{1,0:T(8,128)S(1)}, f32[16,640]{1,0:T(8,128)}, u32[]{:S(2)}) copy-start(f32[16,640]{1,0:T(8,128)} %param.35) | copy-start | bytes 122884
  414.4 1415.0 %copy-start.56 = (f32[640,16]{0,1:T(8,128)S(1)}, f32[640,16]{0,1:T(8,128)}, u32[]{:S(2)}) copy-start(f32[640,16]{0,1:T(8,128)} %param.34) | copy-start | bytes 122884
  414.4 2056.2 %copy-start.57 = (f32[640,16]{0,1:T(8,128)S(1)}, f32[640,16]{0,1:T(8,128)}, u32[]{:S(2)}) copy-start(f32[640,16]{0,1:T(8,128)} %param.33) | copy-start | bytes 122884
  552.5 2173.1 %copy-start.51 = (f32[5,256]{1,0:T(8,128)}, f32[5,256]{1,0:T(8,128)S(1)}, u32[]{:S(2)}) copy-start(f32[5,256]{1,0:T(8,128)S(1)} %get-tuple-element.90) | copy-start | bytes 15364
  554.4 2173.5 %copy-start.52 = (f32[5,256]{1,0:T(8,128)}, f32[5,256]{1,0:T(8,128)S(1)}, u32[]{:S(2)}) copy-start(f32[5,256]{1,0:T(8,128)S(1)} %get-tuple-element.87) | copy-start | bytes 15364
  556.4 2175.9 %copy-start.46 = (f32[640,8]{0,1:T(8,128)}, f32[640,8]{0,1:T(8,128)S(1)}, u32[]{:S(2)}) copy-start(f32[640,8]{0,1:T(8,128)S(1)} %get-tuple-element.93) | copy-start | bytes 61444
  558.3 2176.4 %copy-start.47 = (f32[8,640]{1,0:T(8,128)}, f32[8,640]{1,0:T(8,128)S(1)}, u32[]{:S(2)}) copy-start(f32[8,640]{1,0:T(8,128)S(1)} %get-tuple-element.84) | copy-start | bytes 61444
  1190.3 1552.3 %copy-start.41 = (f32[16,640]{1,0:T(8,128)}, f32[16,640]{1,0:T(8,128)S(1)}, u32[]{:S(2)}) copy-start(f32[16,640]{1,0:T(8,128)S(1)} %get-tuple-element.78) | copy-start | bytes 122884
  1830.9 909.4 %copy-start.42 = (f32[640,16]{0,1:T(8,128)}, f32[640,16]{0,1:T(8,128)S(1)}, u32[]{:S(2)}) copy-start(f32[640,16]{0,1:T(8,128)S(1)} %get-tuple-element.80) | copy-start | bytes 122884
  2562.6 360.4 %all-reduce.21.cloned.1.call-start = ((), (), s32[]{:S(2)}) async-start(), calls=%async_computation.13 | async-start | bytes 17432576 | tf_op jit(solution)/shard_map/psum | solution.py:56
  2759.6 362.0 %all-reduce.19.cloned.1.call-start = ((), (), s32[]{:S(2)}) async-start(), calls=%async_computation.12 | async-start | bytes 17432576 | tf_op jit(solution)/shard_map/psum | solution.py:56
  2958.4 361.6 %all-reduce.17.cloned.1.call-start = ((), (), s32[]{:S(2)}) async-start(), calls=%async_computation.11 | async-start | bytes 17432576 | tf_op jit(solution)/shard_map/psum | solution.py:56
  (72 other events, 2408.0 us)
Sparse Core Ops, SparseCore 0:
  11.4 67.5 all-gather.8
  82.3 61.5 all-gather.10
  147.7 63.0 all-gather.14
  214.4 62.9 all-gather.12
  280.9 62.9 all-gather.16
  392.1 158.4 all-reduce.24
  553.5 635.3 reduce-scatter.8
  1192.0 637.4 reduce-scatter.6
  1832.4 638.1 reduce-scatter.4
  2562.7 161.5 all-reduce.22
  2759.7 163.2 all-reduce.20
  2958.6 162.9 all-reduce.18
  3156.9 163.1 all-reduce.16
where the time goes:
time: 3360 us; the launch traced here: 3350 us
  waiting for transfers between devices  2880 us (86%)
  matrix products  231 us (7%)
  blocking collectives  172 us (5%)
    psum x4, waiting for transfers between devices, sharded_grams(): lax.psum((partial_grams[0], partial_grams[1], partial_grams[2], partial_g...  641 us
    reduce_scatter x1, waiting for transfers between devices, body(): lax.psum_scatter(gate_local, ('fsdp', 'ctx'), scatter_dimension=1, tiled=...  640 us
    reduce_scatter x1, waiting for transfers between devices, body(): lax.psum_scatter(up_local, ('fsdp', 'ctx'), scatter_dimension=1, tiled=True)  639 us
    reduce_scatter x1, waiting for transfers between devices, body(): lax.psum_scatter(down_local, ('fsdp', 'ctx'), scatter_dimension=0, tiled=...  631 us
    unnamed x14, waiting for transfers between devices  134 us
    psum x1, blocking collectives, body(): lax.psum((jnp.sum(fresh[0] * fresh[0]), jnp.sum(fresh[1] * fresh[1]), jnp...  69.7 us
  transfers between devices with their start and end apart: 15, of which 14 were waited for; matrix products, arithmetic and copies ran while one was open for 2% of the time, Pallas kernels for 0%

commit v1 on v0

v1 whole, which is shorter than its diff:
```python
import itertools
import math

import jax
import jax.numpy as jnp
import numpy as np
from jax import lax
from jax.experimental import pallas as pl
from jax.experimental.pallas import tpu as pltpu
from jax.sharding import PartitionSpec as P

HQ = 4
HD = 256
D = 640
FF = 2048
WINDOW = 512
NS_ITERS = 4
ADAM_STEP = 10
DEVICES = 128

NORM_EPS = 1e-06
ORTHO_EPS = 1e-07
POLY_FIRST = 3.4445
POLY_SECOND = -4.775
POLY_THIRD = 2.0315
MOMENTUM = 0.95
MUON_RATE = 0.6
MUON_DECAY = 0.01
ADAM_RATE = 0.7
BETA_FIRST = 0.9
BETA_SECOND = 0.999
ADAM_EPS = 1e-08

AXES = ("fsdp", "ctx")
MESH = pl.DeviceIdType.MESH
ALL = slice(None)
BF = jnp.bfloat16
F32 = jnp.float32

CORE = 6
WIDTHS = (3 * D, D + HD)
CUBES = ((1, 5, 3), (0, 2, 4))
PIECES = (
    (1, 0, 256, 0, 0),
    (1, 256, 128, 0, 1),
    (1, 384, 128, 0, 2),
    (1, 512, 128, 1, 0),
    (1, 640, 128, 1, 1),
    (1, 768, 128, 1, 2),
    (0, 0, 256, 2, 0),
    (0, 256, 384, 2, 1),
    (0, 640, 256, 2, 2),
    (0, 896, 384, 3, 0),
    (0, 1280, 384, 3, 1),
    (0, 1664, 256, 3, 2),
)
GROUPS = ((1, 0, 512, 0), (1, 512, 384, 1), (0, 0, 896, 0), (0, 896, 1024, 1))
COUNT = len(PIECES)
PAIR = (0, 1, 2, 3)
SMALL = (4, 5)
ATTENTION = PAIR + SMALL
FEED = tuple(range(6, COUNT))


def cube_of(piece):
    return GROUPS[piece[3]][3]


NEAR, FAR = CUBES
BLOCKS = tuple((r, c) for r in range(5) for c in range(r, 5))


def order_of(piece):
    return tuple(CUBES[1 - cube_of(piece)][(piece[4] + step) % 3] for step in range(3))


def place():
    f = lax.axis_index("fsdp")
    c = lax.axis_index("ctx")
    return f // 2, (f % 2) * 2 + c // 8, (c // 2) % 4, c % 2


def gray(v):
    return v // 2, (v % 2 + v // 2) % 2


def place_bits(x, z, y, core):
    return gray(x) + gray(z) + gray(y) + (core,)


def partner(where, bits):
    x, z, y, core = where
    for bit in bits:
        if bit == 0:
            x = 3 - x
        elif bit == 1:
            x = x + 1 - 2 * (x % 2)
        elif bit == 2:
            z = 3 - z
        elif bit == 3:
            z = z + 1 - 2 * (z % 2)
        elif bit == 4:
            y = 3 - y
        elif bit == 5:
            y = y + 1 - 2 * (y % 2)
        else:
            core = 1 - core
    return (x * 2 + z // 2, (z % 2) * 8 + y * 2 + core)


def greet(peers):
    barrier = pltpu.get_barrier_semaphore()
    for peer in peers:
        pl.semaphore_signal(barrier, inc=1, device_id=peer, device_id_type=MESH)


def greeted(peers):
    pl.semaphore_wait(pltpu.get_barrier_semaphore(), len(peers))


def remote(src, dst, send_sem, recv_sem, peer):
    return pltpu.make_async_remote_copy(
        src_ref=src,
        dst_ref=dst,
        send_sem=send_sem,
        recv_sem=recv_sem,
        device_id=peer,
        device_id_type=MESH,
    )


def dot_nn(a, b):
    return jnp.dot(a, b, preferred_element_type=F32)


def dot_nt(a, b):
    return lax.dot_general(a, b, (((1,), (1,)), ((), ())), preferred_element_type=F32)


def dot_tn(a, b):
    return lax.dot_general(a, b, (((0,), (0,)), ((), ())), preferred_element_type=F32)


def parts_of(value):
    high = value.astype(BF)
    return high, (value - high.astype(F32)).astype(BF)


def dot_exact(rows, pair):
    high, low = parts_of(rows)
    count = rows.shape[0]
    both = dot_nn(jnp.concatenate([high, low], axis=0), pair[0])
    return both[:count] + both[count:] + dot_nn(high, pair[1])


def fresh_of(grad_rows, moment):
    return MOMENTUM * moment + grad_rows


def inverse_rms(values):
    return lax.rsqrt(jnp.mean(values * values, axis=-1, keepdims=True) + NORM_EPS)


GELU_RATE = math.sqrt(2.0 / math.pi)
GELU_CUBE = 0.044715
TOKENS = 512


def block_kernel(*refs):
    x_ref, cot_hbm = refs[0:2]
    wq, wk, wv, wo, wg, wu, wd = refs[2:9]
    gains_ref, select_hbm, lane_mask, turn = refs[9:13]
    moments = refs[13:20]
    out_hbm, input_grad_hbm = refs[20:22]
    sums, ortho = refs[22:24], refs[24]
    weights, core_in, arrive, owns = refs[25:27], refs[27:29], refs[29:31], refs[31:33]
    (
        pair_own,
        small_own,
        x_prev,
        cot,
        select,
        low,
        query_full,
        output_full,
        key_value_full,
        gain_rows,
        query,
        window,
        probs,
        wide,
        window_cot,
        back_in,
        blocks,
        blocks_in,
        blocks_arrive,
        blocks_whole,
        rows_in,
        rows_out,
    ) = refs[33:55]
    (
        load_sems,
        own_sems,
        send_sems,
        recv_sems,
        pass_send,
        pass_recv,
        half_send,
        half_recv,
        sum_send,
        sum_recv,
        direct_send,
        direct_recv,
        last_send,
        last_recv,
        edge_send,
        edge_recv,
        far_send,
        far_recv,
        block_send,
        block_recv,
        whole_send,
        whole_recv,
        whole_pass_send,
        whole_pass_recv,
        back_send,
        back_recv,
    ) = refs[55:]
    feed_buffer, pair_buffer = weights
    out, middle, second_cot = (wide.at[512 * n : 512 * n + 512] for n in range(3))
    where = place()
    mine = place_bits(*where)
    core = mine[CORE]
    peers = [partner(where, (bit,)) for bit in range(7)]
    f, c = lax.axis_index("fsdp"), lax.axis_index("ctx")
    after, before = (f, (c + 1) % 16), (f, (c + 15) % 16)
    masks = [tuple(n for n in range(3) if mask // (4, 2, 1)[n] % 2) for mask in range(1, 8)]
    far_bits = [tuple(FAR[n] for n in chosen) for chosen in masks]
    near_bits = [tuple(NEAR[n] for n in chosen) for chosen in masks]
    far_peers = [partner(where, bits) for bits in far_bits]
    near_peers = [partner(where, bits) for bits in near_bits]
    met = peers + [after, before]
    met += [peer for peer, bits in zip(far_peers, far_bits) if len(bits) > 1]
    met += [peer for peer, bits in zip(near_peers, near_bits) if len(bits) > 1]
    greet(met)

    loads = [
        pltpu.make_async_copy(cot_hbm, cot, load_sems.at[0]),
        pltpu.make_async_copy(select_hbm, select, load_sems.at[1]),
    ]
    for copy in loads:
        copy.start()
    pair_own[0:8] = wq[...]
    pair_own[8:16] = wo[...]
    small_own[...] = jnp.zeros_like(small_own)
    small_own[0:5] = dot_nn(wk[...].astype(BF), turn[...])
    small_own[8:13] = dot_nn(wv[...].astype(BF), turn[...])
    small_own[5:6, 0:5] = gains_ref[0:1]
    small_own[5:6, 128:133] = gains_ref[1:2]
    for n, value in enumerate((wg, wu, wd)):
        owns[0][:, n * D : n * D + D] = value[...].astype(BF)
    owns[1][:, 0:D] = pair_own[...].astype(BF)
    owns[1][:, D:] = small_own[...].astype(BF)
    greeted(met)

    edge = remote(x_ref, x_prev, edge_send.at[0], edge_recv.at[0], after)
    edge.start()

    local = []
    for array in range(2):
        copy = pltpu.make_async_copy(owns[array], weights[array].at[mine], own_sems.at[array])
        copy.start()
        local.append(copy)
    gather_sends, passed = ({n: [] for n in range(COUNT)} for _ in range(2))
    direct_sends = {}
    gather_steps = {}

    def gathered(n, free, other=None):
        array, first, count = PIECES[n][:3]
        index = tuple(
            ALL if bit in free else (1 - mine[bit] if bit == other else mine[bit])
            for bit in range(7)
        )
        return weights[array].at[index + (ALL, pl.ds(first, count))]

    def pass_on(n, slot, part):
        copy = remote(part, part, pass_send.at[n, slot], pass_recv.at[n, slot], peers[CORE])
        copy.start()
        passed[n].append(copy)

    cube_bits = (near_bits, far_bits)
    cube_peers = (near_peers, far_peers)

    def gather_start(group):
        array, first, count, cube = GROUPS[group]
        columns = pl.ds(first, count)
        direct_sends[group] = []
        for k in range(7):
            copy = remote(
                owns[array].at[:, columns],
                weights[array].at[mine + (ALL, columns)],
                direct_send.at[group, k],
                direct_recv.at[group, k],
                cube_peers[cube][k],
            )
            copy.start()
            direct_sends[group].append(copy)

    def gather_step(n, step):
        order, direct = order_of(PIECES[n]), CUBES[cube_of(PIECES[n])]
        if step > 0:
            gather_steps[n].wait_recv()
        elif n % 3 == 0:
            for copy in direct_sends[n // 3]:
                copy.wait_recv()
        if step < 3:
            part = gathered(n, direct + order[:step])
            copy = remote(
                part, part, send_sems.at[n, step], recv_sems.at[n, step], peers[order[step]]
            )
            copy.start()
            gather_sends[n].append(copy)
            gather_steps[n] = copy
        if step == 1:
            pass_on(n, 0, gathered(n, direct + order[:1]))
        elif step > 1:
            pass_on(n, step - 1, gathered(n, direct + order[: step - 1], order[step - 1]))

    def all_passed(numbers):
        for n in numbers:
            for copy in passed[n]:
                copy.wait_recv()

    for group in range(4):
        gather_start(group)
    for copy in local:
        copy.wait()
    for step in range(3):
        for n in range(COUNT):
            gather_step(n, step)
    for n in ATTENTION:
        gather_step(n, 3)
    for copy in loads:
        copy.wait()
    edge.wait()
    all_passed(ATTENTION)

    small = pair_buffer[(ALL,) * 8 + (slice(D, D + HD),)].reshape(DEVICES, 16, HD).astype(F32)
    rows = jnp.concatenate(
        [small[:, 0:8].reshape(1024, HD), small[:, 8:16].reshape(1024, HD)], axis=1
    ).astype(BF)
    key_value_full[...] = dot_nn(select[0:D], rows).astype(BF)
    lanes = lane_mask[0].astype(F32) + lane_mask[1].astype(F32)
    gain_lanes = (dot_nn(select[D:], rows[:, 0:HD]) * lanes).astype(BF)
    half_of = lax.broadcasted_iota(jnp.int32, (8, HD), 1) // 128
    chooser = (half_of == lax.broadcasted_iota(jnp.int32, (8, HD), 0)).astype(F32).astype(BF)
    gain_rows[...] = dot_nt(chooser, gain_lanes)
    attn_gain, feed_gain = gain_rows[0:1], gain_rows[1:2]

    def normalize(i, carry):
        rows = pl.ds(pl.multiple_of(i * 128, 128), 128)
        for source, target in ((x_prev, x_prev), (x_ref, low)):
            value = source[rows].astype(F32)
            target[rows] = (value * inverse_rms(value) * attn_gain).astype(BF)
        return carry

    lax.fori_loop(0, 4, normalize, 0)

    def project(i, carry):
        rows = pl.ds(pl.multiple_of(i * 256, 256), 256)
        own_rows = pl.ds(pl.multiple_of(TOKENS + i * 256, 256), 256)
        window[rows] = dot_nn(x_prev[rows], key_value_full[...]).astype(BF)
        window[own_rows] = dot_nn(low[rows], key_value_full[...]).astype(BF)
        return carry

    lax.fori_loop(0, 2, project, 0)
    def head_rows(head):
        return pl.ds(pl.multiple_of(head * HD, HD), HD)

    def unpack(head, carry):
        both = pair_buffer[(head // 2, head % 2) + (ALL,) * 6 + (slice(0, D),)]
        both = both.reshape(32, 16, D).astype(F32)
        rows = head_rows(head)
        query_full[rows] = both[:, 0:8].reshape(HD, D).astype(BF)
        output_full[rows] = both[:, 8:16].reshape(HD, D).astype(BF)
        query[head] = dot_nt(low[...], query_full[rows]).astype(BF)
        return carry

    lax.fori_loop(0, HQ, unpack, 0)

    absent = jnp.where(c == 0, -1e30, 0.0).astype(F32)
    score_scale = 1.0 / math.sqrt(HD)

    def upper():
        row = lax.broadcasted_iota(jnp.int32, (512, 256), 0) % 256
        return lax.broadcasted_iota(jnp.int32, (512, 256), 1) > row

    def spread(ends, inner):
        above = jnp.where(upper(), ends, 0.0)
        return jnp.concatenate([above, inner, ends - above], axis=1).astype(BF)

    def attend(b):
        def pair_of_heads(hp, carry):
            heads, rows = pl.ds(2 * hp, 2), slice(256 * b, 256 * b + 256)
            keys = window[256 * b : 256 * b + 768, 0:HD]
            values = window[256 * b : 256 * b + 768, HD:]
            scores = dot_nt(query[heads, rows].reshape(512, HD), keys) * score_scale
            ends = jnp.where(upper(), scores[:, 0:256] + absent, scores[:, 512:])
            inner = scores[:, 256:512]
            if b == 0:
                inner = inner + absent
            top = jnp.maximum(
                jnp.max(ends, axis=-1, keepdims=True), jnp.max(inner, axis=-1, keepdims=True)
            )
            ends, inner = jnp.exp(ends - top), jnp.exp(inner - top)
            total = jnp.sum(ends, axis=-1, keepdims=True) + jnp.sum(inner, axis=-1, keepdims=True)
            ends, inner = ends * (1.0 / total), inner * (1.0 / total)
            probs[2 * b + hp, :, 0:256] = ends
            probs[2 * b + hp, :, 256:] = inner
            mixed = dot_nn(spread(ends, inner), values).astype(BF)
            columns = pl.ds(pl.multiple_of(hp * 512, 512), 512)
            select[rows, columns] = jnp.concatenate([mixed[:256], mixed[256:]], axis=1)
            return carry

        lax.fori_loop(0, 2, pair_of_heads, 0)

    attend(0)
    attend(1)
    for n in FEED:
        gather_step(n, 3)
    def all_sent(numbers):
        for n in numbers:
            for copy in gather_sends[n] + passed[n]:
                copy.wait_send()
            if n % 3 == 0:
                for copy in direct_sends[n // 3]:
                    copy.wait_send()

    all_sent(ATTENTION)

    def second_norm(i, carry):
        rows = pl.ds(pl.multiple_of(i * 256, 256), 256)
        value = x_ref[rows].astype(F32) + dot_nn(select[rows], output_full[...])
        middle[rows] = value
        out[rows] = value
        second_cot[rows] = jnp.zeros((256, D), F32)
        normed = (value * inverse_rms(value) * feed_gain).astype(BF)
        pair_buffer[(0, 0, i) + (ALL,) * 5 + (slice(0, D),)] = normed.reshape((2,) * 4 + (16, D))
        return carry

    lax.fori_loop(0, 2, second_norm, 0)
    all_passed(FEED)
    all_sent(FEED)

    sum_sends, sum_steps, sum_directs = [], {}, {}

    def halve(number):
        if isinstance(number, int) and number >= 4:
            array, lead = 1, (ALL,) * 6
            columns = pl.ds(0, D) if number == 4 else pl.ds(D, HD)
        else:
            array, lead, columns = 0, (number // 2, number % 2) + (ALL,) * 4, ALL
        return remote(
            weights[array].at[lead + (1 - core, ALL, columns)],
            core_in[array].at[lead + (ALL, columns)],
            half_send.at[number],
            half_recv.at[number],
            peers[CORE],
        )

    def sum_send_step(n, step):
        array, first, count = PIECES[n][:3]
        order = order_of(PIECES[n])
        bit = order[step]
        source = tuple(
            mine[b] if b in order[:step] else (1 - mine[b] if b == bit else ALL) for b in range(6)
        )
        target = tuple(mine[b] if b in order[: step + 1] else ALL for b in range(6))
        tail = (ALL, pl.ds(first, count))
        copy = remote(
            weights[array].at[source + (core,) + tail],
            arrive[array].at[target + tail],
            sum_send.at[n, step],
            sum_recv.at[n, step],
            peers[bit],
        )
        copy.start()
        sum_sends.append(copy)
        sum_steps[n] = copy

    def add(into, other, free):
        turns = max(free - 3, 0)

        def some(i, carry):
            lead = tuple(i // 2 ** (turns - 1 - n) % 2 for n in range(turns))
            for index in itertools.product((0, 1), repeat=free - turns):
                into[lead + index] = into[lead + index] + other[lead + index]
            return carry

        if turns > 0:
            lax.fori_loop(0, 2**turns, some, 0)
        else:
            some(0, 0)

    def first_sums(numbers, halves):
        for number in halves:
            half_copies[number].wait_recv()
        for n in numbers:
            array, first, count = PIECES[n][:3]
            tail = (ALL, pl.ds(first, count))
            add(
                weights[array].at[(ALL,) * 6 + (core,) + tail],
                core_in[array].at[(ALL,) * 6 + tail],
                6,
            )
            sum_send_step(n, 0)

    def next_sums(numbers, step):
        for n in numbers:
            array, first, count = PIECES[n][:3]
            order = order_of(PIECES[n])
            bit = order[step]
            tail = (ALL, pl.ds(first, count))
            sum_steps[n].wait_recv()
            here = tuple(mine[b] if b in order[: step + 1] else ALL for b in range(6))
            there = tuple(1 - mine[b] if b == bit else v for b, v in enumerate(here))
            into, other = weights[array].at[here + (core,) + tail], arrive[array].at[there + tail]
            add(into, other, 5 - step)
            if step < 2:
                sum_send_step(n, step + 1)

    def flipped(bits):
        return tuple(1 - mine[b] if b in bits else mine[b] for b in range(6))

    def sum_direct(group):
        array, first, count, cube = GROUPS[group]
        tail = (ALL, pl.ds(first, count))
        sum_directs[group] = []
        for k, bits in enumerate(cube_bits[cube]):
            copy = remote(
                weights[array].at[flipped(bits) + (core,) + tail],
                arrive[array].at[mine[:6] + tail],
                last_send.at[group, k],
                last_recv.at[group, k],
                cube_peers[cube][k],
            )
            copy.start()
            sum_sends.append(copy)
            sum_directs[group].append(copy)

    def last_sums(group):
        array, first, count, cube = GROUPS[group]
        tail = (ALL, pl.ds(first, count))
        total = weights[array][mine[:6] + (core,) + tail].astype(F32)
        for k, bits in enumerate(cube_bits[cube]):
            sum_directs[group][k].wait_recv()
            total = total + arrive[array][flipped(bits) + tail].astype(F32)
        sums[array][:, pl.ds(first, count)] = total

    def feed(j, carry):
        gate_at, up_at, down_at = (
            (j // 2, j % 2) + (ALL,) * 6 + (slice(n * D, n * D + D),) for n in range(3)
        )
        gate_rows = feed_buffer[gate_at].reshape(512, D)
        up_rows = feed_buffer[up_at].reshape(512, D)
        down_rows = feed_buffer[down_at].reshape(512, D)
        second_low = pair_buffer[(0, 0) + (ALL,) * 6 + (slice(0, D),)].reshape(TOKENS, D)
        hidden, gate_cot, up_cot = [], [], []
        for part in range(2):
            tokens = slice(256 * part, 256 * part + 256)
            gate = dot_nt(second_low[tokens], gate_rows)
            up = dot_nt(second_low[tokens], up_rows)
            hidden_cot = dot_nt(cot[tokens], down_rows)
            square = gate * gate
            bend = jnp.tanh(GELU_RATE * gate * (1.0 + GELU_CUBE * square))
            half = 0.5 * (1.0 + bend)
            gelu = gate * half
            slope = half + 0.5 * gate * (1.0 - bend * bend) * (
                GELU_RATE * (1.0 + 3.0 * GELU_CUBE * square)
            )
            hidden.append((gelu * up).astype(BF))
            gate_cot.append((hidden_cot * up * slope).astype(BF))
            up_cot.append((hidden_cot * gelu).astype(BF))
            out[tokens] += dot_nn(hidden[part], down_rows)
            second_cot[tokens] += dot_nn(gate_cot[part], gate_rows) + dot_nn(up_cot[part], up_rows)
        hidden, gate_cot, up_cot = (
            jnp.concatenate(parts, axis=0) for parts in (hidden, gate_cot, up_cot)
        )
        shape = (2,) * 5 + (16, D)
        feed_buffer[down_at] = dot_tn(hidden, cot[...]).astype(BF).reshape(shape)
        feed_buffer[gate_at] = dot_tn(gate_cot, second_low).astype(BF).reshape(shape)
        feed_buffer[up_at] = dot_tn(up_cot, second_low).astype(BF).reshape(shape)
        halve(j).start()
        return carry

    lax.fori_loop(0, 4, feed, 0)
    half_copies = [halve(number) for number in range(6)]

    stores = [pltpu.make_async_copy(out, out_hbm, load_sems.at[2])]
    stores[0].start()

    def second_back(i, total):
        rows = pl.ds(pl.multiple_of(i * 128, 128), 128)
        value = middle[rows]
        rms = inverse_rms(value)
        direct = second_cot[rows]
        total = total + jnp.sum(direct * value * rms, axis=0, keepdims=True)
        scaled = direct * feed_gain
        inner = jnp.mean(value * scaled, axis=-1, keepdims=True)
        value = cot[rows].astype(F32) + rms * scaled - value * (rms * rms * rms * inner)
        middle[rows] = value
        x_prev[rows] = value.astype(BF)
        return total

    feed_gain_cot = lax.fori_loop(0, 4, second_back, jnp.zeros((1, D), F32))

    def output_back(head, carry):
        rows = head_rows(head)
        select[TOKENS : 2 * TOKENS, rows] = dot_nt(x_prev[...], output_full[rows]).astype(BF)
        output_full[rows] = dot_tn(select[0:TOKENS, rows], x_prev[...]).astype(BF)
        return carry

    lax.fori_loop(0, HQ, output_back, 0)
    window_cot[...] = jnp.zeros_like(window_cot)

    def attend_back(b):
        def pair_of_heads(hp, carry):
            heads, rows = pl.ds(2 * hp, 2), slice(256 * b, 256 * b + 256)
            span = slice(256 * b, 256 * b + 768)
            keys, values = window[span, 0:HD], window[span, HD:]
            columns = pl.ds(pl.multiple_of(hp * 512, 512), 512)
            below = slice(TOKENS + 256 * b, TOKENS + 256 * b + 256)
            given = select[below, columns]
            given = jnp.concatenate([given[:, :HD], given[:, HD:]], axis=0)
            ends, inner = probs[2 * b + hp, :, 0:256], probs[2 * b + hp, :, 256:]
            prob_cot = dot_nt(given, values)
            ends_cot = jnp.where(upper(), prob_cot[:, 0:256], prob_cot[:, 512:])
            inner_cot = prob_cot[:, 256:512]
            total = jnp.sum(ends_cot * ends, axis=-1, keepdims=True) + jnp.sum(
                inner_cot * inner, axis=-1, keepdims=True
            )
            score_low = spread(ends * (ends_cot - total), inner * (inner_cot - total))
            query_cot = (dot_nn(score_low, keys) * score_scale).astype(BF)
            select[below, columns] = jnp.concatenate([query_cot[:256], query_cot[256:]], axis=1)
            window_cot[span, 0:HD] += dot_tn(score_low, query[heads, rows].reshape(512, HD))
            window_cot[span, HD:] += dot_tn(spread(ends, inner), given)
            return carry

        lax.fori_loop(0, 2, pair_of_heads, 0)

    def send_back(half):
        rows = slice(256 * half, 256 * half + 256)
        window[rows, 0:HD] = (window_cot[rows, 0:HD] * score_scale).astype(BF)
        window[rows, HD:] = window_cot[rows, HD:].astype(BF)
        copy = remote(
            window.at[rows], back_in.at[rows], edge_send.at[1 + half], edge_recv.at[1 + half], before
        )
        copy.start()
        return copy

    attend_back(0)
    backs = [send_back(0)]
    first_sums(FEED, range(4))
    attend_back(1)
    backs.append(send_back(1))

    def query_back(head, carry):
        rows = head_rows(head)
        both = jnp.concatenate(
            [
                dot_tn(select[TOKENS : 2 * TOKENS, rows], low[...]).reshape(32, 8, D),
                output_full[rows].astype(F32).reshape(32, 8, D),
            ],
            axis=1,
        )
        pair_buffer[(head // 2, head % 2) + (ALL,) * 6 + (slice(0, D),)] = (
            both.astype(BF).reshape((2,) * 5 + (16, D))
        )
        return carry

    lax.fori_loop(0, HQ, query_back, 0)
    half_copies[4].start()

    def first_back(i, carry):
        rows = pl.ds(pl.multiple_of(i * 256, 256), 256)
        below = pl.ds(pl.multiple_of(TOKENS + i * 256, 256), 256)
        second_cot[rows] = dot_nn(select[below], query_full[...])
        return carry

    lax.fori_loop(0, 2, first_back, 0)
    again = pltpu.make_async_copy(select_hbm, select, load_sems.at[1])
    again.start()
    first_sums(PAIR, (4,))
    for copy in backs:
        copy.wait()
    returned = back_in[...].astype(F32)
    edge_low = jnp.concatenate(
        [
            window_cot[TOKENS:, 0:HD] * score_scale + returned[:, 0:HD],
            window_cot[TOKENS:, HD:] + returned[:, HD:],
        ],
        axis=1,
    ).astype(BF)
    window[TOKENS:] = edge_low
    key_value_grad = dot_tn(low[...], edge_low).astype(BF)

    def first_gain(i, total):
        rows = pl.ds(pl.multiple_of(i * 256, 256), 256)
        own_rows = pl.ds(pl.multiple_of(TOKENS + i * 256, 256), 256)
        direct = second_cot[rows] + dot_nt(window[own_rows], key_value_full[...])
        second_cot[rows] = direct
        value = x_ref[rows].astype(F32)
        return total + jnp.sum(direct * value * inverse_rms(value), axis=0, keepdims=True)

    attn_gain_cot = lax.fori_loop(0, 2, first_gain, jnp.zeros((1, D), F32))

    def as_columns(row):
        return dot_tn(jnp.broadcast_to(row, (8, D)), jnp.full((8, HD), 0.125, F32))

    gain_cots = as_columns(attn_gain_cot) * lane_mask[0].astype(F32) + as_columns(
        feed_gain_cot
    ) * lane_mask[1].astype(F32)
    again.wait()
    key_value_rows = dot_tn(select[0:D], key_value_grad)
    gain_cot_rows = dot_tn(select[D:], gain_cots.astype(BF))
    both = jnp.concatenate(
        [
            (key_value_rows[:, 0:HD] + gain_cot_rows).reshape(DEVICES, 8, HD),
            key_value_rows[:, HD:].reshape(DEVICES, 8, HD),
        ],
        axis=1,
    )
    pair_buffer[(ALL,) * 8 + (slice(D, D + HD),)] = both.astype(BF).reshape((2,) * 7 + (16, HD))
    half_copies[5].start()
    next_sums(FEED, 0)
    next_sums(PAIR, 0)

    def input_back(i, carry):
        rows = pl.ds(pl.multiple_of(i * 128, 128), 128)
        value = x_ref[rows].astype(F32)
        rms = inverse_rms(value)
        scaled = second_cot[rows] * attn_gain
        inner = jnp.mean(value * scaled, axis=-1, keepdims=True)
        second_cot[rows] = middle[rows] + rms * scaled - value * (rms * rms * rms * inner)
        return carry

    first_sums(SMALL, (5,))
    lax.fori_loop(0, 4, input_back, 0)
    stores.append(pltpu.make_async_copy(second_cot, input_grad_hbm, load_sems.at[3]))
    stores[1].start()
    next_sums(FEED, 1)
    next_sums(PAIR, 1)
    next_sums(SMALL, 0)
    next_sums(FEED, 2)
    sum_direct(2)
    sum_direct(3)
    next_sums(PAIR, 2)
    sum_direct(0)
    next_sums(SMALL, 1)
    next_sums(SMALL, 2)
    sum_direct(1)
    last_sums(2)
    last_sums(3)
    last_sums(0)
    last_sums(1)
    small = sums[1][:, D:]
    natural = lax.dot_general(
        small,
        turn[...].astype(F32),
        (((1,), (1,)), ((), ())),
        precision=lax.Precision.HIGHEST,
        preferred_element_type=F32,
    )
    gain_row = lax.broadcasted_iota(jnp.int32, (16, HD), 0) == 5
    sums[1][:, D:] = jnp.where(gain_row, small, natural)
    for copy in stores:
        copy.wait()

    now, outgo, result = wide.at[0:D], wide.at[D : D + 128], wide.at[D + 128 : D + 256]
    outgo[...] = jnp.zeros((128, D), F32)
    for n in range(3):
        outgo[16 * n : 16 * n + 16] = fresh_of(sums[0][:, n * D : n * D + D], moments[4 + n][...])
    outgo[48:56] = fresh_of(sums[1][0:8, 0:D], moments[0][...])
    outgo[72:80] = fresh_of(sums[1][8:16, 0:D], moments[3][...])
    outgo[80:85, 0:HD] = fresh_of(sums[1][0:5, D:], moments[1][...])
    outgo[96:101, 0:HD] = fresh_of(sums[1][8:13, D:], moments[2][...])
    rows_out[...] = outgo[...].astype(BF)
    group = mine[0] * 4 + mine[2] * 2 + mine[4]

    def far_group(bits):
        flipped = [1 - mine[bit] if bit in bits else mine[bit] for bit in FAR]
        return flipped[0] * 4 + flipped[1] * 2 + flipped[2]

    def sixteen(ref, number):
        return ref.at[pl.ds(pl.multiple_of(number * 16, 16), 16)]

    copies = []
    for n, bits in enumerate(far_bits):
        copy = remote(
            sixteen(rows_out, far_group(bits)),
            sixteen(rows_in, group),
            far_send.at[n],
            far_recv.at[n],
            far_peers[n],
        )
        copy.start()
        copies.append(copy)
    sixteen(rows_in, group)[...] = sixteen(rows_out, group)[...]
    for copy in copies:
        copy.wait_recv()
    rows = rows_in[...]

    def block_at(number):
        return (number // 8, number // 4 % 2, number // 2 % 2, number % 2)

    for r in range(5):
        strip = dot_tn(rows[:, 128 * r : 128 * r + 128], rows[:, 128 * r :])
        for number, (row, column) in enumerate(BLOCKS):
            if row == r:
                at = 128 * (column - r)
                blocks[block_at(number)] = strip[:, at : at + 128]
    blocks[block_at(15)] = jnp.zeros((128, 128), F32)
    near_mine = tuple(mine[bit] for bit in NEAR)

    def near_of(bits):
        return tuple(1 - mine[bit] if bit in bits else mine[bit] for bit in NEAR)

    halves = remote(
        blocks.at[1 - core], blocks_in, block_send.at[7], block_recv.at[7], peers[CORE]
    )
    halves.start()
    halves.wait()
    blocks[core] = blocks[core] + blocks_in[...]
    block_copies = []
    for n, bits in enumerate(near_bits):
        copy = remote(
            blocks.at[(core,) + near_of(bits)],
            blocks_arrive.at[near_mine],
            block_send.at[n],
            block_recv.at[n],
            near_peers[n],
        )
        copy.start()
        block_copies.append(copy)
    total = blocks[(core,) + near_mine]
    for copy in block_copies:
        copy.wait_recv()
    for n, bits in enumerate(near_bits):
        total = total + blocks_arrive[near_of(bits)]
    own_block = blocks_whole.at[(core,) + near_mine]
    own_block[...] = total
    whole_copies, whole_passed = [], []

    def whole_pass(n, part):
        copy = remote(
            part, part, whole_pass_send.at[n], whole_pass_recv.at[n], peers[CORE]
        )
        copy.start()
        whole_passed.append(copy)

    for n, bits in enumerate(near_bits):
        copy = remote(own_block, own_block, whole_send.at[n], whole_recv.at[n], near_peers[n])
        copy.start()
        whole_copies.append(copy)
    whole_pass(7, own_block)
    for n, bits in enumerate(near_bits):
        whole_copies[n].wait_recv()
        whole_pass(n, blocks_whole.at[(core,) + near_of(bits)])
    for copy in whole_passed:
        copy.wait_recv()
    square_sum = jnp.zeros((1, 1), F32)
    same = lax.broadcasted_iota(jnp.int32, (128, 128), 0) == lax.broadcasted_iota(
        jnp.int32, (128, 128), 1
    )
    for number, (row, column) in enumerate(BLOCKS):
        if row == column:
            diagonal = jnp.where(same, blocks_whole[block_at(number)], 0.0)
            square_sum = square_sum + jnp.sum(
                jnp.sum(diagonal, axis=0, keepdims=True), axis=1, keepdims=True
            )
    factor = 1.0 / (jnp.sqrt(square_sum) + ORTHO_EPS)
    for number, (row, column) in enumerate(BLOCKS):
        part = blocks_whole[block_at(number)] * (factor * factor)
        now[128 * row : 128 * row + 128, 128 * column : 128 * column + 128] = part
        if row != column:
            now[128 * column : 128 * column + 128, 128 * row : 128 * row + 128] = part.T
    result[...] = rows_in[...].astype(F32) * factor
    gram_high, gram_low = select.at[0:D, 0:D], select.at[D : 2 * D, 0:D]
    poly_high, poly_low = query_full.at[0:D], output_full.at[0:D]
    gram_high[...] = now[...].astype(BF)

    def iterate(_, carry):
        change = POLY_SECOND * now[...] + POLY_THIRD * dot_nn(gram_high[...], gram_high[...])
        poly_high[...] = change.astype(BF)
        result[...] = POLY_FIRST * result[...] + dot_nn(result[...].astype(BF), poly_high[...])
        product = POLY_FIRST * now[...] + dot_nn(gram_high[...], poly_high[...])
        gram_low[...] = product.astype(BF)
        later = POLY_FIRST * product + dot_nn(gram_low[...], poly_high[...])
        now[...] = later
        gram_high[...] = later.astype(BF)
        return carry

    lax.fori_loop(0, NS_ITERS - 2, iterate, 0)
    gram_value = now[...]
    change = POLY_SECOND * gram_value + POLY_THIRD * dot_nn(gram_high[...], gram_high[...])
    poly_high[...], poly_low[...] = parts_of(change)
    gram_low[...] = (gram_value - gram_high[...].astype(F32)).astype(BF)
    gram, poly = (gram_high[...], gram_low[...]), (poly_high[...], poly_low[...])
    value = POLY_FIRST * result[...] + dot_exact(result[...], poly)

    def times_next_gram(rows):
        rows = dot_exact(rows, gram)
        rows = POLY_FIRST * rows + dot_exact(rows, poly)
        return POLY_FIRST * rows + dot_exact(rows, poly)

    once = times_next_gram(value)
    for copy in copies:
        copy.wait_send()
    rows_out[...] = (
        POLY_FIRST * value + POLY_SECOND * once + POLY_THIRD * times_next_gram(once)
    ).astype(BF)
    copies = []
    for n, bits in enumerate(far_bits):
        copy = remote(
            sixteen(rows_out, far_group(bits)),
            ortho.at[group],
            back_send.at[n],
            back_recv.at[n],
            far_peers[n],
        )
        copy.start()
        copies.append(copy)
    ortho[group] = sixteen(rows_out, group)[...]
    for copy in copies:
        copy.wait()
    for copy in block_copies + whole_copies + whole_passed:
        copy.wait_send()
    for copy in half_copies:
        copy.wait_send()
    for copy in sum_sends:
        copy.wait_send()


def block_constants():
    swap = np.array([0, 1, 3, 2])
    position = np.arange(DEVICES).reshape(4, 4, 4, 2)[swap][:, swap][:, :, swap].reshape(DEVICES)
    select = np.zeros((2 * D, 8 * DEVICES), np.float32)
    lane_mask = np.zeros((2, D, HD), np.float32)
    for i in range(D):
        select[i, position[i // 5] * 8 + i % 5] = 1.0
        select[D + i, position[i // 5] * 8 + 5] = 1.0
        lane_mask[0, i, i % 5] = 1.0
        lane_mask[1, i, 128 + i % 5] = 1.0
    index = np.arange(HD).reshape(4, 4, 16)[swap][:, swap].reshape(HD)
    turn = np.eye(HD, dtype=np.float32)[:, index]
    return tuple(jnp.asarray(part, BF) for part in (select, lane_mask, turn))


def block(inputs, cotangent, masters, norm_gains, moments):
    select, lane_mask, turn = block_constants()
    vmem = pl.BlockSpec(memory_space=pltpu.VMEM)
    anywhere = pl.BlockSpec(memory_space=pl.ANY)
    dma = pltpu.SemaphoreType.DMA
    halves = [pltpu.VMEM((2,) * 6 + (16, width), BF) for width in WIDTHS]
    results = pl.pallas_call(
        block_kernel,
        out_shape=[jax.ShapeDtypeStruct((TOKENS, D), F32)] * 2
        + [jax.ShapeDtypeStruct((16, width), F32) for width in WIDTHS]
        + [jax.ShapeDtypeStruct((8, 16, D), BF)],
        in_specs=[vmem, anywhere] + [vmem] * 8 + [anywhere, vmem, vmem] + [vmem] * 7,
        out_specs=[anywhere] * 2 + [vmem] * 3,
        scratch_shapes=[pltpu.VMEM((2,) * 7 + (16, width), BF) for width in WIDTHS]
        + halves
        + halves
        + [pltpu.VMEM((16, width), BF) for width in WIDTHS]
        + [
            pltpu.VMEM((16, D), F32),
            pltpu.VMEM((16, HD), F32),
            pltpu.VMEM((TOKENS, D), BF),
            pltpu.VMEM((TOKENS, D), BF),
            pltpu.VMEM((2 * D, 8 * DEVICES), BF),
            pltpu.VMEM((TOKENS, D), BF),
            pltpu.VMEM((HQ * HD, D), BF),
            pltpu.VMEM((HQ * HD, D), BF),
            pltpu.VMEM((D, 2 * HD), BF),
            pltpu.VMEM((8, D), F32),
            pltpu.VMEM((HQ, TOKENS, HD), BF),
            pltpu.VMEM((2 * TOKENS, 2 * HD), BF),
            pltpu.VMEM((4, 512, 512), F32),
            pltpu.VMEM((3 * TOKENS, D), F32),
            pltpu.VMEM((2 * TOKENS, 2 * HD), F32),
            pltpu.VMEM((TOKENS, 2 * HD), BF),
            pltpu.VMEM((2, 2, 2, 2, 128, 128), F32),
            pltpu.VMEM((2, 2, 2, 128, 128), F32),
            pltpu.VMEM((2, 2, 2, 128, 128), F32),
            pltpu.VMEM((2, 2, 2, 2, 128, 128), F32),
            pltpu.VMEM((128, D), BF),
            pltpu.VMEM((128, D), BF),
            dma((4,)),
            dma((2,)),
            dma((COUNT, 3)),
            dma((COUNT, 3)),
            dma((COUNT, 3)),
            dma((COUNT, 3)),
            dma((6,)),
            dma((6,)),
            dma((COUNT, 3)),
            dma((COUNT, 3)),
            dma((4, 7)),
            dma((4, 7)),
            dma((4, 7)),
            dma((4, 7)),
            dma((3,)),
            dma((3,)),
            dma((7,)),
            dma((7,)),
            dma((8,)),
            dma((8,)),
            dma((7,)),
            dma((7,)),
            dma((8,)),
            dma((8,)),
            dma((7,)),
            dma((7,)),
        ],
        compiler_params=pltpu.CompilerParams(
            collective_id=0, has_side_effects=True, vmem_limit_bytes=59 * 2**20
        ),
        name="block",
    )(inputs, cotangent, *masters, norm_gains, select, lane_mask, turn, *moments)
    return results[0:2], results[2:4], results[4]


SIZES = ((D, HQ * HD), (D, HD), (D, HD), (HQ * HD, D), (D, FF), (D, FF), (FF, D))


def finish_kernel(*refs):
    feed, rest, ortho = refs[:3]
    moments, masters, gains, large = refs[3:10], refs[10:17], refs[17:20], refs[20:22]
    grad_outs, moment_outs, master_outs, gain_outs, large_outs = (
        refs[22:29],
        refs[29:36],
        refs[36:43],
        refs[43:47],
        refs[47:49],
    )
    held, sems = refs[49:51]
    copies = [
        pltpu.make_async_copy(large[n], held.at[n], sems.at[n]) for n in range(2)
    ]
    for copy in copies:
        copy.start()
    stores = []
    for n in range(2):
        copies[n].wait()
        stores.append(pltpu.make_async_copy(held.at[n], large_outs[n], sems.at[2 + n]))
        stores[n].start()
    own = (
        rest[0:8, 0:D],
        rest[0:5, D:],
        rest[8:13, D:],
        rest[8:16, 0:D],
        feed[:, 0:D],
        feed[:, D : 2 * D],
        feed[:, 2 * D :],
    )
    turned = tuple(ortho[n].astype(F32) for n in range(7))
    turned = (
        turned[3][0:8],
        turned[5][0:5, 0:HD],
        turned[6][0:5, 0:HD],
        turned[4][8:16],
        turned[0],
        turned[1],
        turned[2],
    )
    for n in range(7):
        rows, columns = SIZES[n]
        ratio = math.sqrt(max(rows, columns) / rows)
        grad_outs[n][...] = own[n]
        moment_outs[n][...] = fresh_of(own[n], moments[n][...])
        master_outs[n][...] = (
            masters[n][...] * (1.0 - MUON_RATE * MUON_DECAY) - MUON_RATE * ratio * turned[n]
        )
    gain_grads = jnp.concatenate([rest[5:6, D : D + 5], rest[5:6, D + 128 : D + 133]], axis=0)
    norm_gains, gain_first, gain_second = (ref[...] for ref in gains)
    first_moments = BETA_FIRST * gain_first + (1.0 - BETA_FIRST) * gain_grads
    second_moments = BETA_SECOND * gain_second + (1.0 - BETA_SECOND) * gain_grads * gain_grads
    first_hat = first_moments / (1.0 - BETA_FIRST**ADAM_STEP)
    second_hat = second_moments / (1.0 - BETA_SECOND**ADAM_STEP)
    gain_outs[0][...] = gain_grads
    gain_outs[1][...] = first_moments
    gain_outs[2][...] = second_moments
    gain_outs[3][...] = norm_gains - ADAM_RATE * first_hat / (jnp.sqrt(second_hat) + ADAM_EPS)
    for copy in stores:
        copy.wait()


def finish(grads, ortho, moments, masters, gains, large):
    shapes = [jax.ShapeDtypeStruct(moment.shape, F32) for moment in moments]
    vmem = pl.BlockSpec(memory_space=pltpu.VMEM)
    anywhere = pl.BlockSpec(memory_space=pl.ANY)
    return pl.pallas_call(
        finish_kernel,
        out_shape=shapes * 3
        + [jax.ShapeDtypeStruct((2, 5), F32)] * 4
        + [jax.ShapeDtypeStruct((TOKENS, D), F32)] * 2,
        in_specs=[vmem] * 20 + [anywhere] * 2,
        out_specs=[vmem] * 25 + [anywhere] * 2,
        scratch_shapes=[pltpu.VMEM((2, TOKENS, D), F32), pltpu.SemaphoreType.DMA((4,))],
        name="finish",
    )(*grads, ortho, *moments, *masters, *gains, *large)


def body(
    inputs,
    cotangent,
    query_weight,
    key_weight,
    value_weight,
    output_weight,
    gate_weight,
    up_weight,
    down_weight,
    norm_gains,
    query_moment,
    key_moment,
    value_moment,
    output_moment,
    gate_moment,
    up_moment,
    down_moment,
    gain_first,
    gain_second,
):
    moments = (
        query_moment.T,
        key_moment,
        value_moment,
        output_moment,
        gate_moment.T,
        up_moment.T,
        down_moment,
    )
    masters = (
        query_weight.T,
        key_weight,
        value_weight,
        output_weight,
        gate_weight.T,
        up_weight.T,
        down_weight,
    )
    large, grads, ortho = block(inputs, cotangent, masters, norm_gains, moments)
    outs = finish(grads, ortho, moments, masters, (norm_gains, gain_first, gain_second), large)

    def natural(seven):
        return tuple(part.T if n in (0, 4, 5) else part for n, part in enumerate(seven))

    return (
        tuple(outs[25:27])
        + natural(outs[0:7])
        + natural(outs[7:14])
        + natural(outs[14:21])
        + tuple(outs[21:25])
    )


def solution(mesh):
    rows, columns = P(AXES, None), P(None, AXES)
    seven = (columns, rows, rows, rows, columns, columns, rows)
    return jax.shard_map(
        body,
        mesh=mesh,
        in_specs=(rows, rows) + seven + (columns,) + seven + (columns, columns),
        out_specs=(rows, rows) + seven * 3 + (columns,) * 4,
        check_vma=False,
    )
```

time: 3360 us -> 177 us (0.05)
  waiting for transfers between devices: 2880 us -> 0 us
  matrix products: 231 us -> 0 us
  Pallas kernels: 0 us -> 176 us
  blocking collectives: 172 us -> 0 us
    reduce_scatter x3 -> x0, waiting for transfers between devices: 1910 us -> none  [the longest x1 640 us: body(): lax.psum_scatter(gate_local, ('fsdp', 'ctx'), scatter_dimension=1, tiled=...]
    psum x4 -> x0, waiting for transfers between devices: 641 us -> none  [sharded_grams(): lax.psum((partial_grams[0], partial_grams[1], partial_grams[2], partial_g...]
    dot_general x110 -> x0, matrix products: 231 us -> none  [the longest x12 32.4 us: local_gram(): return jnp.dot(current, current.T, precision=HIGH)]
    all_gather x5 -> x0, waiting for transfers between devices: 191 us -> none  [the longest x1 64.1 us: body(): lax.all_gather(up_weight.astype(jnp.bfloat16), ('fsdp', 'ctx'), axis=1, t...]
    pallas_call x0 -> x2, Pallas kernels: none -> 176 us  [the longest x1 171 us: block(): pl.pallas_call(block_kernel, out_shape=[jax.ShapeDtypeStruct((TOKENS, D),...]
    unnamed x14 -> x0, waiting for transfers between devices: 134 us -> none
    all_gather x3 -> x0, blocking collectives: 102 us -> none  [the longest x1 34.3 us: body(): lax.all_gather(norm_gains.astype(jnp.bfloat16), ('fsdp', 'ctx'), axis=1,...]
    psum x1 -> x0, blocking collectives: 69.7 us -> none  [body(): lax.psum((jnp.sum(fresh[0] * fresh[0]), jnp.sum(fresh[1] * fresh[1]), jnp...]
  transfers between devices with their start and end apart: 15 -> 0, of which waited for: 14 -> 0; matrix products, arithmetic and copies ran while one was open for 2% -> 0% of each run, Pallas kernels for 0% -> 0%
where the time goes in v1:
time: 177 us; the launch traced here: 176 us
  Pallas kernels  176 us (99%)
    pallas_call x1, Pallas kernels, block(): pl.pallas_call(block_kernel, out_shape=[jax.ShapeDtypeStruct((TOKENS, D),...  171 us
    pallas_call x1, Pallas kernels, finish(): pl.pallas_call(finish_kernel, out_shape=shapes * 3 + [jax.ShapeDtypeStruc...  4.94 us

profile of v1, /device:TPU:1, one launch (start us, length us, event | category | flops | bytes accessed | tf_op | source)
XLA Modules:
  0.0 176.4 jit_solution(14736881160736432612)
XLA Ops:
  0.7 170.6 %block.1 = (f32[512,640]{1,0:T(8,128)}, f32[512,640]{1,0:T(8,128)}, f32[16,1920]{1,0:T(8,128)}, f32[16,896]{1,0:T(8,128)}, bf16[8,16,640]{2,1,0:T(8,128)(2,1)}) custom-call(bf16[512,640]{1,0:T(8,128)(2,1)} %refs_0_.1, bf16[512,640]{1,0:T(8,128)(2,1)} %refs_1_.1, f32[8,640]{1,0:T(8,128)} %bitcast.23, f32[5,256]{1,0:T(8,128)} %refs_11_.2, f32[5,256]{1,0:T(8,128)} %refs_12_.2, ...), custom_call_target="tpu_custom_call" | custom-call | tf_op jit(solution)/shard_map/block/pallas_call | solution.py:965
  171.3 4.9 %finish.1 = (f32[8,640]{1,0:T(8,128)}, f32[5,256]{1,0:T(8,128)}, f32[5,256]{1,0:T(8,128)}, f32[8,640]{1,0:T(8,128)}, f32[16,640]{1,0:T(8,128)}, /*index=5*/f32[1...) custom-call(f32[16,1920]{1,0:T(8,128)} %get-tuple-element.59.refs_0_, ...), custom_call_target="tpu_custom_call" | custom-call | tf_op jit(solution)/shard_map/finish/pallas_call | solution.py:1103

commit v2 on v1

--- a/solution.py
+++ b/solution.py
@@ -660,9 +660,9 @@
 
     attend_back(0)
     backs = [send_back(0)]
-    first_sums(FEED, range(4))
     attend_back(1)
     backs.append(send_back(1))
+    first_sums(FEED, range(4))
 
     def query_back(head, carry):
         rows = head_rows(head)
@@ -732,8 +732,6 @@
     )
     pair_buffer[(ALL,) * 8 + (slice(D, D + HD),)] = both.astype(BF).reshape((2,) * 7 + (16, HD))
     half_copies[5].start()
-    next_sums(FEED, 0)
-    next_sums(PAIR, 0)
 
     def input_back(i, carry):
         rows = pl.ds(pl.multiple_of(i * 128, 128), 128)
@@ -744,8 +742,10 @@
         second_cot[rows] = middle[rows] + rms * scaled - value * (rms * rms * rms * inner)
         return carry
 
+    lax.fori_loop(0, 4, input_back, 0)
     first_sums(SMALL, (5,))
-    lax.fori_loop(0, 4, input_back, 0)
+    next_sums(FEED, 0)
+    next_sums(PAIR, 0)
     stores.append(pltpu.make_async_copy(second_cot, input_grad_hbm, load_sems.at[3]))
     stores[1].start()
     next_sums(FEED, 1)

time: 177 us -> 175 us (0.989)
  Pallas kernels: 176 us -> 174 us
    pallas_call x1, Pallas kernels: 171 us -> 169 us  [block(): pl.pallas_call(block_kernel, out_shape=[jax.ShapeDtypeStruct((TOKENS, D),...]
where the time goes in v2:
time: 175 us
  Pallas kernels  174 us (99%)
    pallas_call x1, Pallas kernels, block(): pl.pallas_call(block_kernel, out_shape=[jax.ShapeDtypeStruct((TOKENS, D),...  169 us
    pallas_call x1, Pallas kernels, finish(): pl.pallas_call(finish_kernel, out_shape=shapes * 3 + [jax.ShapeDtypeStruc...  4.94 us

profile of v2, /device:TPU:1, one launch (start us, length us, event | category | flops | bytes accessed | tf_op | source)
XLA Modules:
  0.0 174.6 jit_solution(11077994558088669576)
XLA Ops:
  0.7 168.8 %block.1 = (f32[512,640]{1,0:T(8,128)}, f32[512,640]{1,0:T(8,128)}, f32[16,1920]{1,0:T(8,128)}, f32[16,896]{1,0:T(8,128)}, bf16[8,16,640]{2,1,0:T(8,128)(2,1)}) custom-call(bf16[512,640]{1,0:T(8,128)(2,1)} %refs_0_.1, bf16[512,640]{1,0:T(8,128)(2,1)} %refs_1_.1, f32[8,640]{1,0:T(8,128)} %bitcast.23, f32[5,256]{1,0:T(8,128)} %refs_11_.2, f32[5,256]{1,0:T(8,128)} %refs_12_.2, ...), custom_call_target="tpu_custom_call" | custom-call | tf_op jit(solution)/shard_map/block/pallas_call | solution.py:965
  169.5 4.9 %finish.1 = (f32[8,640]{1,0:T(8,128)}, f32[5,256]{1,0:T(8,128)}, f32[5,256]{1,0:T(8,128)}, f32[8,640]{1,0:T(8,128)}, f32[16,640]{1,0:T(8,128)}, /*index=5*/f32[1...) custom-call(f32[16,1920]{1,0:T(8,128)} %get-tuple-element.59.refs_0_, ...), custom_call_target="tpu_custom_call" | custom-call | tf_op jit(solution)/shard_map/finish/pallas_call | solution.py:1103
